TPU v7x, 256 devices: a whole 4x4x8 slice. The times are simulated.
256 devices in a mesh: grp: 8 (over z_lo, core), dev: 32 (over z_hi, x, y).
Axes of the slice: x: 4, y: 4, z: 8 (z_hi: 2, z_lo: 4; z = z_hi * 4 + z_lo), core: 2. Of those that a mesh axis runs over, the one named last changes fastest.
Arguments:
- matrix_slab: float32 [32, 1048576], P(None, ('grp', 'dev')), may hold values from -6 to 6
- sign_flips: int32 [1048576], P(('grp', 'dev')), may hold values from 0 to 1
- sample_offset: int32 [4096], P(('grp', 'dev')), may hold values from 0 to 4095, as said below
Outputs:
- transformed: float32 [32, 1048576], P(None, ('grp', 'dev'))
- sketch: float32 [32, 4096], P(None, ('grp', 'dev'))
- gram_matrix: float32 [32, 32], replicated
Inputs may be any that keep to these rules, and one draw needn't show every extreme that they name: Entry k selects row (k // 16) * 4096 + sample_offset[k] of the transform; rows may repeat.
All inputs are finite; a program needn't handle non-finite values.
Results may differ from a plain program's by a relative error of at most 0.00011.
Values sent between devices are 32-bit elements; how exact they have to be, the bound alone decides.
A program may use at most 64 MiB of HBM per device.

v0:
```python
import math

import jax
import jax.numpy as jnp
from jax import lax
from jax.sharding import PartitionSpec as P


def partner_2(block, axis, distance):
    count = lax.axis_size(axis)
    route = []
    for low in range(count):
        high = low | 1 << distance
        if high != low and high < count:
            route += [(low, high), (high, low)]
    return lax.ppermute(block, axis, route)


def hadamard_table(order):
    numbers = jnp.arange(order, dtype=jnp.int32)
    common_bits = numbers[:, None] & numbers[None, :]
    parity = jnp.zeros((order, order), dtype=jnp.int32)
    for position in range(max(order.bit_length() - 1, 0)):
        parity = parity + (common_bits >> position & 1)
    return (1 - 2 * (parity % 2)).astype(jnp.float32)


def mix_local(values):
    columns = values.shape[0]
    local_rows = values.shape[1]
    outer = local_rows // 128
    shaped = values.reshape(columns, outer, 128)
    shaped = jnp.einsum("cak,zk->caz", shaped, hadamard_table(128), precision=lax.Precision.HIGHEST)
    shaped = jnp.einsum(
        "cak,za->czk", shaped, hadamard_table(outer), precision=lax.Precision.HIGHEST
    )
    return shaped


def local(matrix_slab, sign_flips, sample_offset):
    columns = matrix_slab.shape[0]
    local_rows = matrix_slab.shape[1]
    group_count = lax.axis_size("grp")
    dev_count = lax.axis_size("dev")
    total_rows = local_rows * group_count * dev_count
    scaling = jnp.float32(1.0 / math.sqrt(total_rows))
    signs = (1 - 2 * sign_flips).astype(jnp.float32)
    current = mix_local(matrix_slab * signs[None, :])
    dev_place = lax.axis_index("dev")
    for bit_number in range(dev_count.bit_length() - 1):
        partner = partner_2(current, "dev", bit_number)
        lower_side = dev_place >> bit_number & 1 == 0
        current = jnp.where(lower_side, current + partner, partner - current)
    grp_place = lax.axis_index("grp")
    for bit_number in range(group_count.bit_length() - 1):
        partner = partner_2(current, "grp", bit_number)
        lower_side = grp_place >> bit_number & 1 == 0
        current = jnp.where(lower_side, current + partner, partner - current)
    transformed = (current * scaling).reshape(columns, local_rows)
    sketch = jnp.take(transformed, sample_offset, axis=1)
    gram_local = jnp.dot(
        sketch, sketch.T, precision=lax.Precision.HIGHEST, preferred_element_type=jnp.float32
    )
    gram_total = lax.psum(gram_local, ("grp", "dev"))
    sample_total = sample_offset.shape[0] * group_count * dev_count
    gram_matrix = gram_total / jnp.float32(sample_total)
    return (transformed, sketch, gram_matrix)


def solution(mesh):
    return jax.shard_map(
        local,
        mesh=mesh,
        in_specs=(P(None, ("grp", "dev")), P(("grp", "dev")), P(("grp", "dev"))),
        out_specs=(P(None, ("grp", "dev")), P(None, ("grp", "dev")), P()),
        check_vma=False,
    )
```

profile of v0, /device:TPU:1, one launch (start us, length us, event | category | flops | bytes accessed | tf_op | source)
XLA Modules:
  0.0 207.5 jit_solution(13869708146029447496)
XLA Ops:
  0.6 0.7 subtract_convert_fusion
  1.4 1.1 multiply_bitcast_fusion
  2.4 0.1 copy.7
  2.5 0.6 fusion.5
  3.2 0.6 convolution_bitcast_fusion
  3.8 2.2 %collective-permute-start = (f32[32,32,128]{2,1,0:T(8,128)S(1)}, f32[32,32,128]{2,1,0:T(8,128)S(1)}, u32[]{:S(2)}, u32[]{:S(2)}) collective-permute-start(f32[32,32,128]{2,1,0:T(8,128)S(1)} %convolution_bitcast_fusion), channel_id=1, source_target_pairs={{0,1},{1,0},{2,3},{3,2},{4,5},{5,4},{6,7},{7,6},{8,9},{9,8},{10,11... | collective-permute-start | bytes 1572872 | tf_op jit(solution)/shard_map/ppermute | solution.py:16
  6.0 10.4 %collective-permute-done = f32[32,32,128]{2,1,0:T(8,128)S(1)} collective-permute-done((f32[32,32,128]{2,1,0:T(8,128)S(1)}, f32[32,32,128]{2,1,0:T(8,128)S(1)}, u32[]{:S(2)}, u32[]{:S(2)}) %collective-permute-start) | collective-permute-done | bytes 524320 | tf_op jit(solution)/shard_map/ppermute | solution.py:16
  16.4 0.1 subtract_select_fusion.6
  16.5 4.1 %collective-permute-start.1 = (f32[32,32,128]{2,1,0:T(8,128)S(1)}, f32[32,32,128]{2,1,0:T(8,128)S(1)}, u32[]{:S(2)}, u32[]{:S(2)}) collective-permute-start(f32[32,32,128]{2,1,0:T(8,128)S(1)} %subtract_select_fusion.6), channel_id=1, source_target_pairs={{0,2},{2,0},{1,3},{3,1},{4,6},{6,4},{5,7},{7,5},{8,10},{10,8},{9,1... | collective-permute-start | bytes 1572872 | tf_op jit(solution)/shard_map/ppermute | solution.py:16
  20.6 10.5 %collective-permute-done.1 = f32[32,32,128]{2,1,0:T(8,128)S(1)} collective-permute-done((f32[32,32,128]{2,1,0:T(8,128)S(1)}, f32[32,32,128]{2,1,0:T(8,128)S(1)}, u32[]{:S(2)}, u32[]{:S(2)}) %collective-permute-start.1) | collective-permute-done | bytes 524320 | tf_op jit(solution)/shard_map/ppermute | solution.py:16
  31.1 0.1 subtract_select_fusion.5
  31.2 1.3 collective-permute-start.2
  32.5 9.9 %collective-permute-done.2 = f32[32,32,128]{2,1,0:T(8,128)S(1)} collective-permute-done((f32[32,32,128]{2,1,0:T(8,128)S(1)}, f32[32,32,128]{2,1,0:T(8,128)S(1)}, u32[]{:S(2)}, u32[]{:S(2)}) %collective-permute-start.2) | collective-permute-done | bytes 524320 | tf_op jit(solution)/shard_map/ppermute | solution.py:16
  42.3 0.1 subtract_select_fusion.4
  42.4 2.7 %collective-permute-start.3 = (f32[32,32,128]{2,1,0:T(8,128)S(1)}, f32[32,32,128]{2,1,0:T(8,128)S(1)}, u32[]{:S(2)}, u32[]{:S(2)}) collective-permute-start(f32[32,32,128]{2,1,0:T(8,128)S(1)} %subtract_select_fusion.4), channel_id=1, source_target_pairs={{0,8},{8,0},{1,9},{9,1},{2,10},{10,2},{3,11},{11,3},{4,12},{12,4},... | collective-permute-start | bytes 1572872 | tf_op jit(solution)/shard_map/ppermute | solution.py:16
  45.1 10.3 %collective-permute-done.3 = f32[32,32,128]{2,1,0:T(8,128)S(1)} collective-permute-done((f32[32,32,128]{2,1,0:T(8,128)S(1)}, f32[32,32,128]{2,1,0:T(8,128)S(1)}, u32[]{:S(2)}, u32[]{:S(2)}) %collective-permute-start.3) | collective-permute-done | bytes 524320 | tf_op jit(solution)/shard_map/ppermute | solution.py:16
  55.4 0.1 subtract_select_fusion.3
  55.5 7.1 %collective-permute-start.4 = (f32[32,32,128]{2,1,0:T(8,128)S(1)}, f32[32,32,128]{2,1,0:T(8,128)S(1)}, u32[]{:S(2)}, u32[]{:S(2)}) collective-permute-start(f32[32,32,128]{2,1,0:T(8,128)S(1)} %subtract_select_fusion.3), channel_id=1, source_target_pairs={{0,16},{16,0},{1,17},{17,1},{2,18},{18,2},{3,19},{19,3},{4,20},{20... | collective-permute-start | bytes 1572872 | tf_op jit(solution)/shard_map/ppermute | solution.py:16
  62.6 0.0 copy-start.1
  62.6 9.7 %collective-permute-done.4 = f32[32,32,128]{2,1,0:T(8,128)S(1)} collective-permute-done((f32[32,32,128]{2,1,0:T(8,128)S(1)}, f32[32,32,128]{2,1,0:T(8,128)S(1)}, u32[]{:S(2)}, u32[]{:S(2)}) %collective-permute-start.4) | collective-permute-done | bytes 524320 | tf_op jit(solution)/shard_map/ppermute | solution.py:16
  72.3 0.1 subtract_select_fusion.2
  72.4 5.5 %collective-permute-start.5 = (f32[32,32,128]{2,1,0:T(8,128)S(1)}, f32[32,32,128]{2,1,0:T(8,128)S(1)}, u32[]{:S(2)}, u32[]{:S(2)}) collective-permute-start(f32[32,32,128]{2,1,0:T(8,128)S(1)} %subtract_select_fusion.2), channel_id=1, source_target_pairs={{0,32},{32,0},{64,96},{96,64},{128,160},{160,128},{192,224},{224,1... | collective-permute-start | bytes 1572872 | tf_op jit(solution)/shard_map/ppermute | solution.py:16
  77.9 1.5 collective-permute-done.5
  79.4 0.1 subtract_select_fusion.1
  79.5 9.9 %collective-permute-start.6 = (f32[32,32,128]{2,1,0:T(8,128)S(1)}, f32[32,32,128]{2,1,0:T(8,128)S(1)}, u32[]{:S(2)}, u32[]{:S(2)}) collective-permute-start(f32[32,32,128]{2,1,0:T(8,128)S(1)} %subtract_select_fusion.1), channel_id=1, source_target_pairs={{0,64},{64,0},{32,96},{96,32},{128,192},{192,128},{160,224},{224,1... | collective-permute-start | bytes 1572872 | tf_op jit(solution)/shard_map/ppermute | solution.py:16
  89.5 12.0 %collective-permute-done.6 = f32[32,32,128]{2,1,0:T(8,128)S(1)} collective-permute-done((f32[32,32,128]{2,1,0:T(8,128)S(1)}, f32[32,32,128]{2,1,0:T(8,128)S(1)}, u32[]{:S(2)}, u32[]{:S(2)}) %collective-permute-start.6) | collective-permute-done | bytes 524320 | tf_op jit(solution)/shard_map/ppermute | solution.py:16
  101.5 0.1 subtract_select_fusion
  101.6 2.0 collective-permute-start.7
  103.5 0.0 copy-done.1
  103.6 23.2 %collective-permute-done.7 = f32[32,32,128]{2,1,0:T(8,128)S(1)} collective-permute-done((f32[32,32,128]{2,1,0:T(8,128)S(1)}, f32[32,32,128]{2,1,0:T(8,128)S(1)}, u32[]{:S(2)}, u32[]{:S(2)}) %collective-permute-start.7) | collective-permute-done | bytes 524320 | tf_op jit(solution)/shard_map/ppermute | solution.py:16
  126.7 0.1 select_multiply_fusion
  126.8 0.3 copy.10
  127.2 0.0 copy-start
  127.2 0.6 copy.6
  127.8 0.6 gather_fusion
  128.3 0.3 fusion.31
  128.6 0.7 select_bitcast_fusion
  129.3 77.6 %psum.7 = f32[32,32]{1,0:T(8,128)S(1)} all-reduce(f32[32,32]{1,0:T(8,128)S(1)} %fusion.31), channel_id=1, replica_groups=mesh['grp'=8,'dev'=32] {'grp','dev'}, use_global_device_ids=true, to_apply=%region_0.1 | all-reduce | flops 1024 | bytes 8192 | tf_op jit(solution)/shard_map/psum | solution.py:64
  206.9 0.6 broadcast_multiply_fusion
  207.5 0.0 copy-done
  (3 shorter events, 0.0 us)
Async XLA Ops:
  3.8 12.6 %collective-permute-start = (f32[32,32,128]{2,1,0:T(8,128)S(1)}, f32[32,32,128]{2,1,0:T(8,128)S(1)}, u32[]{:S(2)}, u32[]{:S(2)}) collective-permute-start(f32[32,32,128]{2,1,0:T(8,128)S(1)} %convolution_bitcast_fusion), channel_id=1, source_target_pairs={{0,1},{1,0},{2,3},{3,2},{4,5},{5,4},{6,7},{7,6},{8,9},{9,8},{10,11... | collective-permute-start | bytes 1572872 | tf_op jit(solution)/shard_map/ppermute | solution.py:16
  16.5 14.6 %collective-permute-start.1 = (f32[32,32,128]{2,1,0:T(8,128)S(1)}, f32[32,32,128]{2,1,0:T(8,128)S(1)}, u32[]{:S(2)}, u32[]{:S(2)}) collective-permute-start(f32[32,32,128]{2,1,0:T(8,128)S(1)} %subtract_select_fusion.6), channel_id=1, source_target_pairs={{0,2},{2,0},{1,3},{3,1},{4,6},{6,4},{5,7},{7,5},{8,10},{10,8},{9,1... | collective-permute-start | bytes 1572872 | tf_op jit(solution)/shard_map/ppermute | solution.py:16
  31.2 11.1 %collective-permute-start.2 = (f32[32,32,128]{2,1,0:T(8,128)S(1)}, f32[32,32,128]{2,1,0:T(8,128)S(1)}, u32[]{:S(2)}, u32[]{:S(2)}) collective-permute-start(f32[32,32,128]{2,1,0:T(8,128)S(1)} %subtract_select_fusion.5), channel_id=1, source_target_pairs={{0,4},{4,0},{1,5},{5,1},{2,6},{6,2},{3,7},{7,3},{8,12},{12,8},{9,1... | collective-permute-start | bytes 1572872 | tf_op jit(solution)/shard_map/ppermute | solution.py:16
  42.4 13.0 %collective-permute-start.3 = (f32[32,32,128]{2,1,0:T(8,128)S(1)}, f32[32,32,128]{2,1,0:T(8,128)S(1)}, u32[]{:S(2)}, u32[]{:S(2)}) collective-permute-start(f32[32,32,128]{2,1,0:T(8,128)S(1)} %subtract_select_fusion.4), channel_id=1, source_target_pairs={{0,8},{8,0},{1,9},{9,1},{2,10},{10,2},{3,11},{11,3},{4,12},{12,4},... | collective-permute-start | bytes 1572872 | tf_op jit(solution)/shard_map/ppermute | solution.py:16
  55.5 16.8 %collective-permute-start.4 = (f32[32,32,128]{2,1,0:T(8,128)S(1)}, f32[32,32,128]{2,1,0:T(8,128)S(1)}, u32[]{:S(2)}, u32[]{:S(2)}) collective-permute-start(f32[32,32,128]{2,1,0:T(8,128)S(1)} %subtract_select_fusion.3), channel_id=1, source_target_pairs={{0,16},{16,0},{1,17},{17,1},{2,18},{18,2},{3,19},{19,3},{4,20},{20... | collective-permute-start | bytes 1572872 | tf_op jit(solution)/shard_map/ppermute | solution.py:16
  62.6 40.9 %copy-start.1 = (s32[16]{0:T(128)S(1)}, s32[16]{0:T(128)}, u32[]{:S(2)}) copy-start(s32[16]{0:T(128)} %param.5) | copy-start | bytes 196
  72.4 7.0 %collective-permute-start.5 = (f32[32,32,128]{2,1,0:T(8,128)S(1)}, f32[32,32,128]{2,1,0:T(8,128)S(1)}, u32[]{:S(2)}, u32[]{:S(2)}) collective-permute-start(f32[32,32,128]{2,1,0:T(8,128)S(1)} %subtract_select_fusion.2), channel_id=1, source_target_pairs={{0,32},{32,0},{64,96},{96,64},{128,160},{160,128},{192,224},{224,1... | collective-permute-start | bytes 1572872 | tf_op jit(solution)/shard_map/ppermute | solution.py:16
  79.5 21.9 %collective-permute-start.6 = (f32[32,32,128]{2,1,0:T(8,128)S(1)}, f32[32,32,128]{2,1,0:T(8,128)S(1)}, u32[]{:S(2)}, u32[]{:S(2)}) collective-permute-start(f32[32,32,128]{2,1,0:T(8,128)S(1)} %subtract_select_fusion.1), channel_id=1, source_target_pairs={{0,64},{64,0},{32,96},{96,32},{128,192},{192,128},{160,224},{224,1... | collective-permute-start | bytes 1572872 | tf_op jit(solution)/shard_map/ppermute | solution.py:16
  101.6 25.2 %collective-permute-start.7 = (f32[32,32,128]{2,1,0:T(8,128)S(1)}, f32[32,32,128]{2,1,0:T(8,128)S(1)}, u32[]{:S(2)}, u32[]{:S(2)}) collective-permute-start(f32[32,32,128]{2,1,0:T(8,128)S(1)} %subtract_select_fusion), channel_id=1, source_target_pairs={{0,128},{128,0},{32,160},{160,32},{64,192},{192,64},{96,224},{224,... | collective-permute-start | bytes 1572872 | tf_op jit(solution)/shard_map/ppermute | solution.py:16
  127.2 80.3 %copy-start = (f32[4,8,32,128]{3,1,2,0:T(8,128)}, f32[4,8,32,128]{3,1,2,0:T(8,128)S(1)}, u32[]{:S(2)}) copy-start(f32[4,8,32,128]{3,1,2,0:T(8,128)S(1)} %copy.10) | copy-start | bytes 1572868
where the time goes:
time: 208 us; the launch traced here: 207 us
  waiting for transfers between devices  87.5 us (42%)
  blocking collectives  77.6 us (37%)
  starting transfers between devices  34.7 us (17%)
  other arithmetic  3.87 us (2%)
    ppermute x8, waiting for transfers between devices, partner_2(): return lax.ppermute(block, axis, route)  87.5 us
    psum x1, blocking collectives, local(): gram_total = lax.psum(gram_local, ('grp', 'dev'))  77.6 us
    ppermute x8, starting transfers between devices, partner_2(): return lax.ppermute(block, axis, route)  34.7 us
  transfers between devices with their start and end apart: 8, of which 8 were waited for; matrix products, arithmetic and copies ran while one was open for 0% of the time, Pallas kernels for 0%

commit v1 on v0

v1 whole, which is shorter than its diff:
```python
import functools

import jax
import jax.numpy as jnp
from jax import lax
from jax.experimental import pallas as pl
from jax.experimental.pallas import tpu as pltpu
from jax.sharding import PartitionSpec as P

MESH = pl.DeviceIdType.MESH
LANES = 128
SIDE = 16
COLS = 32
LOCAL = 4096
SAMPLES = 16
TOTAL_SAMPLES = 4096
ROWS = LOCAL * COLS // LANES
SCALE = 2.0**-10
PARTS = ((0, 512, True), (512, 512, False))


def fwht(values):
    values = list(values)
    step = 1
    while step < len(values):
        for low in range(0, len(values), 2 * step):
            for at in range(low, low + step):
                a, b = values[at], values[at + step]
                values[at], values[at + step] = a + b, a - b
        step *= 2
    return values


def tree_sum(values):
    values = list(values)
    while len(values) > 1:
        values = [values[i] + values[i + 1] for i in range(0, len(values), 2)]
    return values[0]


def split(value):
    high = value.astype(jnp.bfloat16)
    low = (value - high.astype(jnp.float32)).astype(jnp.bfloat16)
    return high, low


def hadamard(order, scale):
    shape = (order, order)
    common = lax.broadcasted_iota(jnp.int32, shape, 0) & lax.broadcasted_iota(jnp.int32, shape, 1)
    shift = order // 2
    bits = order.bit_length() - 1
    parity = common & 1
    for position in range(1, bits):
        parity = parity ^ ((common >> position) & 1)
    del shift
    return jnp.where(parity == 1, -scale, scale).astype(jnp.bfloat16)


class Team:
    def __init__(self, grp, dev, along_z):
        self.along_z = along_z
        self.grp, self.high, self.low = grp, dev // 16, dev % 16
        self.me = grp + 8 * self.high if along_z else self.low

    def device(self, index):
        if self.along_z:
            return (index % 8, (index // 8) * 16 + self.low)
        return (self.grp, self.high * 16 + index)

    def peer(self, turn):
        away = (turn + 1) // 2
        return (self.me + 8 + away * (2 * ((turn + 1) % 2) - 1)) % SIDE

    def each(self, body):
        def step(turn, carry):
            body(self.peer(turn))
            return carry

        lax.fori_loop(0, SIDE - 1, step, 0)


def rows_at(index, count):
    return pl.ds(pl.multiple_of(index * count, 8), count)


def exchange(team, src, dst, sems, phase, size):
    def one(index):
        pltpu.make_async_remote_copy(
            src_ref=src.at[rows_at(index, size)],
            dst_ref=dst.at[rows_at(team.me, size)],
            send_sem=sems.at[0, phase],
            recv_sem=sems.at[1, phase],
            device_id=team.device(index),
            device_id_type=MESH,
        ).start()

    team.each(one)
    mine = rows_at(team.me, size)
    dst[mine, :] = src[mine, :]


def arrived(dst, sems, phase, size):
    block = dst.at[pl.ds(0, (SIDE - 1) * size)]
    pltpu.make_async_copy(block, block, sems.at[1, phase]).wait()


def sent(dst, sems, phase, size):
    block = dst.at[pl.ds(0, (SIDE - 1) * size)]
    pltpu.make_async_copy(block, block, sems.at[0, phase]).wait()


def mix(src, dst, size):
    def tile(at, carry):
        values = [src[pl.ds(pl.multiple_of(j * size + at * 8, 8), 8), :] for j in range(SIDE)]
        for j, value in enumerate(fwht(values)):
            dst[pl.ds(pl.multiple_of(j * size + at * 8, 8), 8), :] = value
        return carry

    lax.fori_loop(0, size // 8, tile, 0)


def to_inner(src, dst, size):
    def block(at, carry):
        for half in range(2):
            rows = src[pl.ds(at + half * 8 * size, 8, stride=size), :]
            dst[pl.ds(pl.multiple_of(at * SIDE + half * 8, 8), 8), :] = rows
        return carry

    lax.fori_loop(0, size, block, 0, unroll=8)


def to_outer(src, dst, size):
    def block(at, carry):
        for tile in range(size // 8):
            rows = src[pl.ds(at + tile * 8 * SIDE, 8, stride=SIDE), :]
            dst[pl.ds(pl.multiple_of(at * size + tile * 8, 8), 8), :] = rows
        return carry

    lax.fori_loop(0, SIDE, block, 0, unroll=4)


def gram_of(mid, part, first, outer, inner_along_z, offsets):
    start, count, _ = part
    size = count // SIDE
    lane = lax.broadcasted_iota(jnp.int32, (8, LANES), 1)
    marks = []
    for j in range(SIDE):
        for r in range(size // 16):
            row = start + first * size + outer * (size // 16) + r
            place = ((row // LANES) * 4 + lane // COLS) * LANES + row % LANES
            place = place.astype(jnp.float32)
            for half in range(2):
                if inner_along_z:
                    held = offsets[pl.ds(j * SIDE + half * 8, 8), :]
                else:
                    held = offsets[pl.ds(j + half * 8 * SIDE, 8, stride=SIDE), :]
                marks.append(jnp.where(held == place, 1.0, 0.0))
    marks = jnp.concatenate(marks, axis=0).astype(jnp.bfloat16)
    a = lax.broadcasted_iota(jnp.int32, (LANES, LANES), 0) // COLS
    b = lax.broadcasted_iota(jnp.int32, (LANES, LANES), 1) // COLS
    same = jnp.where(a == b, 1.0, 0.0).astype(jnp.bfloat16)
    counts = jnp.dot(marks, same, preferred_element_type=jnp.float32)
    values = mid[...]
    return lax.dot_general(
        values,
        counts * values,
        (((0,), (0,)), ((), ())),
        precision=lax.Precision.HIGHEST,
        preferred_element_type=jnp.float32,
    )


def kernel(x_any, flips_any, offs_any, out_any, sketch_ref, gram_ref, *scratch):
    (x, flips, offs, mixed, final, out, off_row, off_z, off_plane, off_all, gram_rows, gram_xy,
     gram_z, gram_sum, gram_all, picked, load_sems, store_sems, sems, small_sems) = scratch[:20]
    held = [scratch[20 + 8 * i : 28 + 8 * i] for i in range(len(PARTS))]
    grp, dev = lax.axis_index("grp"), lax.axis_index("dev")
    zs, xy = Team(grp, dev, True), Team(grp, dev, False)

    load_x = pltpu.make_async_copy(x_any, x, load_sems.at[0])
    load_f = pltpu.make_async_copy(flips_any, flips, load_sems.at[1])
    load_o = pltpu.make_async_copy(offs_any, offs, load_sems.at[2])
    load_x.start()
    load_f.start()
    load_o.start()

    barrier = pltpu.get_barrier_semaphore()
    for team in (zs, xy):
        team.each(
            lambda index, team=team: pl.semaphore_signal(
                barrier, inc=1, device_id=team.device(index), device_id_type=MESH
            )
        )

    table = hadamard(LANES, SCALE)
    tables = jnp.concatenate([table, table], axis=1)
    load_f.wait()
    load_x.wait()
    for group in range(COLS // 8):
        values = []
        for blk in range(LOCAL // LANES):
            sign = (1 - 2 * flips[pl.ds(blk, 1), :]).astype(jnp.float32)
            values.append(x[pl.ds(group * 8, 8), pl.ds(blk * LANES, LANES)] * sign)
        for blk, value in enumerate(fwht(values)):
            mixed[pl.ds(blk * COLS + group * 8, 8), :] = value

    def local(part, send):
        start, count, _ = part
        for at in range(0, count, LANES):
            high, low = split(mixed[pl.ds(start + at, LANES), :])
            send[pl.ds(at, LANES), :] = lax.dot_general(
                tables,
                jnp.concatenate([high, low], axis=1),
                (((1,), (1,)), ((), ())),
                preferred_element_type=jnp.float32,
            )

    def teams(i):
        return (zs, xy) if PARTS[i][2] else (xy, zs)

    def size(i):
        return PARTS[i][1] // SIDE

    def scatter_outer(i):
        local(PARTS[i], held[i][0])
        exchange(teams(i)[0], held[i][0], held[i][1], sems, 4 * i, size(i))

    def scatter_inner(i):
        _, got, flat, turned, got_inner, _, _, _ = held[i]
        arrived(got, sems, 4 * i, size(i))
        mix(got, flat, size(i))
        to_inner(flat, turned, size(i))
        exchange(teams(i)[1], turned, got_inner, sems, 4 * i + 1, size(i))

    def return_inner(i):
        got_inner, mid, back = held[i][4:7]
        arrived(got_inner, sems, 4 * i + 1, size(i))
        mix(got_inner, mid, size(i))
        exchange(teams(i)[1], mid, back, sems, 4 * i + 2, size(i))

    def return_outer(i):
        back, flat = held[i][6:8]
        arrived(back, sems, 4 * i + 2, size(i))
        to_outer(back, flat, size(i))
        mine = final.at[pl.ds(PARTS[i][0], PARTS[i][1])]
        exchange(teams(i)[0], flat, mine, sems, 4 * i + 3, size(i))

    def finish(i):
        start, count, _ = PARTS[i]
        arrived(final.at[pl.ds(start, count)], sems, 4 * i + 3, size(i))
        for at in range(start, start + count, LANES):
            block = final[pl.ds(at, LANES), :].T
            for b in range(4):
                out[:, pl.ds((at // LANES * 4 + b) * LANES, LANES)] = block[b * COLS : (b + 1) * COLS]
        columns = pl.ds(start * 4, count * 4)
        pltpu.make_async_copy(out.at[:, columns], out_any.at[:, columns], store_sems.at[i]).start()

    def small(team, index, src, dst, phase):
        pltpu.make_async_remote_copy(
            src_ref=src,
            dst_ref=dst,
            send_sem=small_sems.at[0, phase],
            recv_sem=small_sems.at[1, phase],
            device_id=team.device(index),
            device_id_type=MESH,
        ).start()

    def small_done(block, side, phase):
        pltpu.make_async_copy(block, block, small_sems.at[side, phase]).wait()

    load_o.wait()
    lane = lax.broadcasted_iota(jnp.int32, (1, LANES), 1)
    row = jnp.full((1, LANES), -1, jnp.int32)
    for k in range(SAMPLES):
        row = jnp.where(lane % COLS == k, offs[k], row)
    off_row[...] = row.astype(jnp.float32)[None]

    pl.semaphore_wait(barrier, 2 * (SIDE - 1))

    scatter_outer(0)
    scatter_outer(1)
    zs.each(lambda index: small(zs, index, off_row, off_z.at[pl.ds(zs.me, 1)], 0))
    off_z[pl.ds(zs.me, 1)] = off_row[...]
    scatter_inner(1)
    small_done(off_z.at[pl.ds(0, SIDE - 1)], 1, 0)
    for j in range(SIDE):
        off_plane[pl.ds(j, 1), :] = off_z[j]
    xy.each(lambda index: small(xy, index, off_plane, off_all.at[rows_at(xy.me, SIDE)], 1))
    off_all[rows_at(xy.me, SIDE), :] = off_plane[...]
    scatter_inner(0)
    return_inner(0)
    return_inner(1)

    small_done(off_all.at[pl.ds(0, SIDE * (SIDE - 1))], 1, 1)
    product = tree_sum(
        gram_of(held[i][5], PARTS[i], teams(i)[0].me, teams(i)[1].me, PARTS[i][2], off_all)
        for i in range(len(PARTS))
    )
    lane32 = lax.broadcasted_iota(jnp.int32, (COLS, LANES), 1) // COLS
    folded = tree_sum(
        jnp.where(lane32 == b, product[b * COLS : (b + 1) * COLS], 0.0) for b in range(4)
    )
    folded = folded + pltpu.roll(folded, 64, 1)
    folded = folded + pltpu.roll(folded, 32, 1)
    lane8 = lax.broadcasted_iota(jnp.int32, (8, LANES), 1) // COLS
    packed = tree_sum(
        jnp.where(lane8 == b, folded[b * 8 : (b + 1) * 8], 0.0) for b in range(4)
    )
    packed = packed * (1.0 / TOTAL_SAMPLES)
    for i in range(8):
        gram_rows[i] = packed[i : i + 1]
    xy.each(lambda index: small(xy, index, gram_rows.at[pl.ds(index % 8, 1)], gram_xy.at[pl.ds(xy.me, 1)], 2))
    gram_xy[pl.ds(xy.me, 1)] = gram_rows[pl.ds(xy.me % 8, 1)]

    return_outer(0)

    small_done(gram_xy.at[pl.ds(0, SIDE - 1)], 1, 2)
    gram_sum[0] = tree_sum(gram_xy[j] for j in range(SIDE))
    zs.each(lambda index: small(zs, index, gram_sum.at[pl.ds(0, 1)], gram_z.at[pl.ds(zs.me, 1)], 3))
    gram_z[pl.ds(zs.me, 1)] = gram_sum[pl.ds(0, 1)]

    return_outer(1)

    small_done(gram_z.at[pl.ds(0, SIDE - 1)], 1, 3)
    gram_sum[1] = tree_sum(gram_z[j] for j in range(SIDE))

    def share(turn, carry):
        index = (xy.me // 8) * 8 + (xy.me + turn) % 8
        small(xy, index, gram_sum.at[pl.ds(1, 1)], gram_all.at[pl.ds(xy.me % 8, 1)], 4)
        return carry

    lax.fori_loop(1, 8, share, 0)
    gram_all[pl.ds(xy.me % 8, 1)] = gram_sum[pl.ds(1, 1)]

    finish(1)
    small_done(gram_all.at[pl.ds(0, 7)], 1, 4)
    whole = jnp.concatenate([gram_all[i] for i in range(8)], axis=0)
    for b in range(4):
        turned = pltpu.roll(whole, LANES - COLS * b, 1) if b else whole
        gram_ref[pl.ds(b * 8, 8), :] = turned[:, :COLS]
    finish(0)

    for k in range(SAMPLES):
        at = offs[k]
        value = final[pl.ds((at // 512) * LANES + at % LANES, 1), :]
        picked[pl.ds(k, 1), :] = jnp.where(lane // COLS == (at // LANES) % 4, value, 0.0)
    c = lax.broadcasted_iota(jnp.int32, (COLS, LANES), 0)
    l = lax.broadcasted_iota(jnp.int32, (COLS, LANES), 1)
    sketch_ref[...] = lax.dot_general(
        jnp.where(l % COLS == c, 1.0, 0.0),
        picked[...],
        (((1,), (1,)), ((), ())),
        precision=lax.Precision.HIGHEST,
        preferred_element_type=jnp.float32,
    )

    for i in range(len(PARTS)):
        for phase in range(4):
            sent(held[i][1], sems, 4 * i + phase, size(i))
    small_done(off_z.at[pl.ds(0, SIDE - 1)], 0, 0)
    small_done(off_all.at[pl.ds(0, SIDE * (SIDE - 1))], 0, 1)
    small_done(gram_xy.at[pl.ds(0, SIDE - 1)], 0, 2)
    small_done(gram_z.at[pl.ds(0, SIDE - 1)], 0, 3)
    small_done(gram_all.at[pl.ds(0, 7)], 0, 4)
    for i in range(len(PARTS)):
        columns = pl.ds(PARTS[i][0] * 4, PARTS[i][1] * 4)
        pltpu.make_async_copy(out.at[:, columns], out_any.at[:, columns], store_sems.at[i]).wait()


def local(matrix_slab, sign_flips, sample_offset):
    f32 = jnp.float32
    scratch = [
        pltpu.VMEM((COLS, LOCAL), f32),
        pltpu.VMEM((LOCAL // LANES, LANES), jnp.int32),
        pltpu.SMEM((SAMPLES,), jnp.int32),
        pltpu.VMEM((ROWS, LANES), f32),
        pltpu.VMEM((ROWS, LANES), f32),
        pltpu.VMEM((COLS, LOCAL), f32),
        pltpu.VMEM((1, 1, LANES), f32),
        pltpu.VMEM((SIDE, 1, LANES), f32),
        pltpu.VMEM((SIDE, LANES), f32),
        pltpu.VMEM((SIDE * SIDE, LANES), f32),
        pltpu.VMEM((8, 1, LANES), f32),
        pltpu.VMEM((SIDE, 1, LANES), f32),
        pltpu.VMEM((SIDE, 1, LANES), f32),
        pltpu.VMEM((2, 1, LANES), f32),
        pltpu.VMEM((8, 1, LANES), f32),
        pltpu.VMEM((SAMPLES, LANES), f32),
        pltpu.SemaphoreType.DMA((3,)),
        pltpu.SemaphoreType.DMA((len(PARTS),)),
        pltpu.SemaphoreType.DMA((2, 4 * len(PARTS))),
        pltpu.SemaphoreType.DMA((2, 5)),
    ]
    for _, count, _ in PARTS:
        scratch += [pltpu.VMEM((count, LANES), f32)] * 8
    return pl.pallas_call(
        kernel,
        out_shape=(
            jax.ShapeDtypeStruct((COLS, LOCAL), f32),
            jax.ShapeDtypeStruct((COLS, SAMPLES), f32),
            jax.ShapeDtypeStruct((COLS, COLS), f32),
        ),
        in_specs=[pl.BlockSpec(memory_space=pl.ANY)] * 3,
        out_specs=(
            pl.BlockSpec(memory_space=pl.ANY),
            pl.BlockSpec(memory_space=pltpu.VMEM),
            pl.BlockSpec(memory_space=pltpu.VMEM),
        ),
        scratch_shapes=scratch,
        compiler_params=pltpu.CompilerParams(
            collective_id=0, has_side_effects=True, vmem_limit_bytes=24 << 20
        ),
        name="hadamard",
    )(matrix_slab, sign_flips.reshape(LOCAL // LANES, LANES), sample_offset)


def solution(mesh):
    return jax.shard_map(
        local,
        mesh=mesh,
        in_specs=(P(None, ("grp", "dev")), P(("grp", "dev")), P(("grp", "dev"))),
        out_specs=(P(None, ("grp", "dev")), P(None, ("grp", "dev")), P()),
        check_vma=False,
    )
```

time: 208 us -> 51.6 us (0.25)
  waiting for transfers between devices: 87.5 us -> 0 us
  blocking collectives: 77.6 us -> 0 us
  Pallas kernels: 0 us -> 46 us
  starting transfers between devices: 34.7 us -> 0 us
  other arithmetic: 3.87 us -> 0 us
  local copies, waits for them, and re-layouts: 1.58 us -> 4.47 us
    ppermute x8 -> x0, waiting for transfers between devices: 87.5 us -> none  [partner_2(): return lax.ppermute(block, axis, route)]
    psum x1 -> x0, blocking collectives: 77.6 us -> none  [local(): gram_total = lax.psum(gram_local, ('grp', 'dev'))]
    pallas_call x0 -> x1, Pallas kernels: none -> 46 us  [local(): pl.pallas_call(kernel, out_shape=(jax.ShapeDtypeStruct((COLS, LOCAL), f32...]
    ppermute x8 -> x0, starting transfers between devices: 34.7 us -> none  [partner_2(): return lax.ppermute(block, axis, route)]
    unnamed x6 -> x8, local copies, waits for them, and re-layouts: 0.41 us -> 3.8 us
  transfers between devices with their start and end apart: 8 -> 0, of which waited for: 8 -> 0; matrix products, arithmetic and copies ran while one was open for 0% -> 0% of each run, Pallas kernels for 0% -> 0%
where the time goes in v1:
time: 51.6 us; the launch traced here: 51.1 us
  Pallas kernels  46 us (89%)
  local copies, waits for them, and re-layouts  4.47 us (9%)
  between operations  0.65 us (1%)
    pallas_call x1, Pallas kernels, local(): pl.pallas_call(kernel, out_shape=(jax.ShapeDtypeStruct((COLS, LOCAL), f32...  46 us
    unnamed x8, local copies, waits for them, and re-layouts  3.8 us

profile of v1, /device:TPU:1, one launch (start us, length us, event | category | flops | bytes accessed | tf_op | source)
XLA Modules:
  0.0 51.1 jit_solution(5089465722420031803)
XLA Ops:
  0.6 0.0 copy-start.2
  0.6 0.6 %copy-done.2 = s32[16]{0:T(128)S(1)} copy-done((s32[16]{0:T(128)S(1)}, s32[16]{0:T(128)}, u32[]{:S(2)}) %copy-start.2) | copy-done | bytes 88
  1.3 0.0 copy-start
  1.3 1.0 %copy-done = f32[32,4096]{1,0:T(8,128)S(1)} copy-done((f32[32,4096]{1,0:T(8,128)S(1)}, f32[32,4096]{1,0:T(8,128)}, u32[]{:S(2)}) %copy-start) | copy-done | bytes 524312
  2.3 0.0 copy-start.1
  2.3 0.7 %copy-done.1 = s32[4096]{0:T(1024)S(1)} copy-done((s32[4096]{0:T(1024)S(1)}, s32[4096]{0:T(1024)}, u32[]{:S(2)}) %copy-start.1) | copy-done | bytes 16408
  3.0 46.0 %hadamard.1 = (f32[32,4096]{1,0:T(8,128)S(1)}, f32[32,16]{1,0:T(8,128)S(1)}, f32[32,32]{1,0:T(8,128)S(1)}) custom-call(f32[32,4096]{1,0:T(8,128)S(1)} %copy-done, s32[32,128]{1,0:T(8,128)S(1)} %bitcast.1, s32[16]{0:T(128)S(1)} %copy-done.2), custom_call_target="tpu_custom_call" | custom-call | tf_op jit(solution)/shard_map/hadamard/pallas_call | solution.py:396
  49.0 0.7 %copy.6 = f32[32,16]{0,1:T(8,128)} copy(f32[32,16]{1,0:T(8,128)S(1)} %get-tuple-element.4) | data formatting | bytes 4096 | tf_op jit(solution)/shard_map/hadamard/pallas_call | solution.py:396
  49.7 0.8 %copy.9 = f32[32,4096]{1,0:T(8,128)} copy(f32[32,4096]{1,0:T(8,128)S(1)} %get-tuple-element.9) | data formatting | bytes 1048576
  50.5 0.6 %copy.10 = f32[32,32]{1,0:T(8,128)} copy(f32[32,32]{1,0:T(8,128)S(1)} %get-tuple-element.11) | data formatting | bytes 8192
Async XLA Ops:
  0.6 0.7 %copy-start.2 = (s32[16]{0:T(128)S(1)}, s32[16]{0:T(128)}, u32[]{:S(2)}) copy-start(s32[16]{0:T(128)} %offs_any.1) | copy-start | bytes 196
  1.3 1.0 %copy-start = (f32[32,4096]{1,0:T(8,128)S(1)}, f32[32,4096]{1,0:T(8,128)}, u32[]{:S(2)}) copy-start(f32[32,4096]{1,0:T(8,128)} %x_any.1) | copy-start | bytes 1572868
  2.3 0.7 %copy-start.1 = (s32[4096]{0:T(1024)S(1)}, s32[4096]{0:T(1024)}, u32[]{:S(2)}) copy-start(s32[4096]{0:T(1024)} %param.4) | copy-start | bytes 49156

commit v2 on v1

v2 whole, which is shorter than its diff:
```python
import functools

import jax
import jax.numpy as jnp
from jax import lax
from jax.experimental import pallas as pl
from jax.experimental.pallas import tpu as pltpu
from jax.sharding import PartitionSpec as P

MESH = pl.DeviceIdType.MESH
LANES = 128
SIDE = 16
COLS = 32
LOCAL = 4096
SAMPLES = 16
TOTAL_SAMPLES = 4096
ROWS = LOCAL * COLS // LANES
SCALE = 2.0**-10
PARTS = ((0, 256, True), (256, 256, True), (512, 256, False), (768, 256, False))


def fwht(values):
    values = list(values)
    step = 1
    while step < len(values):
        for low in range(0, len(values), 2 * step):
            for at in range(low, low + step):
                a, b = values[at], values[at + step]
                values[at], values[at + step] = a + b, a - b
        step *= 2
    return values


def tree_sum(values):
    values = list(values)
    while len(values) > 1:
        values = [values[i] + values[i + 1] for i in range(0, len(values), 2)]
    return values[0]


def split(value):
    high = value.astype(jnp.bfloat16)
    low = (value - high.astype(jnp.float32)).astype(jnp.bfloat16)
    return high, low


def hadamard(order, scale):
    shape = (order, order)
    common = lax.broadcasted_iota(jnp.int32, shape, 0) & lax.broadcasted_iota(jnp.int32, shape, 1)
    bits = order.bit_length() - 1
    parity = common & 1
    for position in range(1, bits):
        parity = parity ^ ((common >> position) & 1)
    return jnp.where(parity == 1, -scale, scale).astype(jnp.bfloat16)


class Team:
    def __init__(self, grp, dev, kind):
        self.kind = kind
        self.grp, self.high, self.low = grp, dev // 16, dev % 16
        self.z, self.core = grp // 2 + 4 * self.high, grp % 2
        self.me, self.count = {
            "z": (2 * self.z + self.core, 16),
            "xy": (self.low, 16),
            "plane": (16 * self.core + self.low, 32),
            "line": (self.z, 8),
        }[kind]

    def device(self, index):
        if self.kind == "z":
            return (index % 8, (index // 8) * 16 + self.low)
        if self.kind == "xy":
            return (self.grp, self.high * 16 + index)
        if self.kind == "plane":
            return ((self.grp // 2) * 2 + index // 16, self.high * 16 + index % 16)
        return ((index % 4) * 2 + self.core, (index // 4) * 16 + self.low)

    def peer(self, turn):
        away = (turn + 1) // 2
        return (self.me + self.count // 2 + away * (2 * ((turn + 1) % 2) - 1)) % self.count

    def each(self, body):
        def step(turn, carry):
            body(self.peer(turn))
            return carry

        lax.fori_loop(0, self.count - 1, step, 0)


def rows_at(index, count):
    return pl.ds(pl.multiple_of(index * count, 8), count)


def exchange(team, src, dst, sems, phase, size):
    def one(index):
        pltpu.make_async_remote_copy(
            src_ref=src.at[rows_at(index, size)],
            dst_ref=dst.at[rows_at(team.me, size)],
            send_sem=sems.at[0, phase],
            recv_sem=sems.at[1, phase],
            device_id=team.device(index),
            device_id_type=MESH,
        ).start()

    team.each(one)
    mine = rows_at(team.me, size)
    dst[mine, :] = src[mine, :]


def arrived(dst, sems, phase, size):
    block = dst.at[pl.ds(0, (SIDE - 1) * size)]
    pltpu.make_async_copy(block, block, sems.at[1, phase]).wait()


def sent(dst, sems, phase, size):
    block = dst.at[pl.ds(0, (SIDE - 1) * size)]
    pltpu.make_async_copy(block, block, sems.at[0, phase]).wait()


def mix(src, dst, size):
    def tile(at, carry):
        values = [src[pl.ds(pl.multiple_of(j * size + at * 8, 8), 8), :] for j in range(SIDE)]
        for j, value in enumerate(fwht(values)):
            dst[pl.ds(pl.multiple_of(j * size + at * 8, 8), 8), :] = value
        return carry

    lax.fori_loop(0, size // 8, tile, 0)


def to_inner(src, dst, size):
    def block(at, carry):
        for half in range(2):
            rows = src[pl.ds(at + half * 8 * size, 8, stride=size), :]
            dst[pl.ds(pl.multiple_of(at * SIDE + half * 8, 8), 8), :] = rows
        return carry

    lax.fori_loop(0, size, block, 0, unroll=8)


def to_outer(src, dst, size):
    def block(at, carry):
        for tile in range(size // 8):
            rows = src[pl.ds(at + tile * 8 * SIDE, 8, stride=SIDE), :]
            dst[pl.ds(pl.multiple_of(at * size + tile * 8, 8), 8), :] = rows
        return carry

    lax.fori_loop(0, SIDE, block, 0, unroll=4)


def gram_of(mid, part, first, outer, inner_along_z, offsets):
    start, count, _ = part
    size = count // SIDE
    lane = lax.broadcasted_iota(jnp.int32, (8, LANES), 1)
    marks = []
    for j in range(SIDE):
        for r in range(size // 16):
            row = start + first * size + outer * (size // 16) + r
            place = ((row // LANES) * 4 + lane // COLS) * LANES + row % LANES
            place = place.astype(jnp.float32)
            for half in range(2):
                if inner_along_z:
                    held = offsets[pl.ds(j * SIDE + half * 8, 8), :]
                else:
                    held = offsets[pl.ds(j + half * 8 * SIDE, 8, stride=SIDE), :]
                marks.append(jnp.where(held == place, 1.0, 0.0))
    marks = jnp.concatenate(marks, axis=0).astype(jnp.bfloat16)
    a = lax.broadcasted_iota(jnp.int32, (LANES, LANES), 0) // COLS
    b = lax.broadcasted_iota(jnp.int32, (LANES, LANES), 1) // COLS
    same = jnp.where(a == b, 1.0, 0.0).astype(jnp.bfloat16)
    counts = jnp.dot(marks, same, preferred_element_type=jnp.float32)
    values = mid[...]
    return lax.dot_general(
        values,
        counts * values,
        (((0,), (0,)), ((), ())),
        precision=lax.Precision.HIGHEST,
        preferred_element_type=jnp.float32,
    )


def kernel(x_any, flips_any, offs_any, out, sketch, gram, *scratch):
    (x, flips, offs, mixed, final, off_row, off_z, off_plane, off_all, packed, gram_plane,
     gram_sum, gram_line, load_sems, sems, small_sems) = scratch[:16]
    held = [scratch[16 + 8 * i : 24 + 8 * i] for i in range(len(PARTS))]
    grp, dev = lax.axis_index("grp"), lax.axis_index("dev")
    zs, xy, plane, line = (Team(grp, dev, kind) for kind in ("z", "xy", "plane", "line"))

    load_x = pltpu.make_async_copy(x_any, x, load_sems.at[0])
    load_f = pltpu.make_async_copy(flips_any, flips, load_sems.at[1])
    load_o = pltpu.make_async_copy(offs_any, offs, load_sems.at[2])
    load_f.start()
    load_x.start()
    load_o.start()

    barrier = pltpu.get_barrier_semaphore()
    for team in (zs, plane):
        team.each(
            lambda index, team=team: pl.semaphore_signal(
                barrier, inc=1, device_id=team.device(index), device_id_type=MESH
            )
        )

    def teams(i):
        return (zs, xy) if PARTS[i][2] else (xy, zs)

    def size(i):
        return PARTS[i][1] // SIDE

    def small(team, index, src, dst, phase):
        pltpu.make_async_remote_copy(
            src_ref=src,
            dst_ref=dst,
            send_sem=small_sems.at[0, phase],
            recv_sem=small_sems.at[1, phase],
            device_id=team.device(index),
            device_id_type=MESH,
        ).start()

    def small_done(block, side, phase):
        pltpu.make_async_copy(block, block, small_sems.at[side, phase]).wait()

    table = hadamard(LANES, SCALE)
    tables = jnp.concatenate([table, table], axis=1)
    load_f.wait()
    load_x.wait()
    for group in range(COLS // 8):
        values = []
        for blk in range(LOCAL // LANES):
            sign = (1 - 2 * flips[pl.ds(blk, 1), :]).astype(jnp.float32)
            values.append(x[pl.ds(group * 8, 8), pl.ds(blk * LANES, LANES)] * sign)
        for blk, value in enumerate(fwht(values)):
            mixed[pl.ds(blk * COLS + group * 8, 8), :] = value

    for i, (start, count, _) in enumerate(PARTS):
        for at in range(0, count, LANES):
            high, low = split(mixed[pl.ds(start + at, LANES), :])
            held[i][0][pl.ds(at, LANES), :] = lax.dot_general(
                tables,
                jnp.concatenate([high, low], axis=1),
                (((1,), (1,)), ((), ())),
                preferred_element_type=jnp.float32,
            )

    load_o.wait()
    lane = lax.broadcasted_iota(jnp.int32, (1, LANES), 1)
    row = jnp.full((1, LANES), -1, jnp.int32)
    for k in range(SAMPLES):
        row = jnp.where(lane % COLS == k, offs[k], row)
    off_row[...] = row.astype(jnp.float32)[None]

    pl.semaphore_wait(barrier, zs.count + plane.count - 2)

    def scatter_outer(i):
        exchange(teams(i)[0], held[i][0], held[i][1], sems, 4 * i, size(i))

    def scatter_inner(i):
        _, got, flat, turned, got_inner, _, _, _ = held[i]
        arrived(got, sems, 4 * i, size(i))
        mix(got, flat, size(i))
        to_inner(flat, turned, size(i))
        exchange(teams(i)[1], turned, got_inner, sems, 4 * i + 1, size(i))

    def return_inner(i):
        got_inner, mid, back = held[i][4:7]
        arrived(got_inner, sems, 4 * i + 1, size(i))
        mix(got_inner, mid, size(i))
        exchange(teams(i)[1], mid, back, sems, 4 * i + 2, size(i))

    def return_outer(i):
        back, flat = held[i][6:8]
        arrived(back, sems, 4 * i + 2, size(i))
        to_outer(back, flat, size(i))
        mine = final.at[pl.ds(PARTS[i][0], PARTS[i][1])]
        exchange(teams(i)[0], flat, mine, sems, 4 * i + 3, size(i))

    def finish(i):
        start, count, _ = PARTS[i]
        arrived(final.at[pl.ds(start, count)], sems, 4 * i + 3, size(i))
        for at in range(start, start + count, LANES):
            block = final[pl.ds(at, LANES), :].T
            for b in range(4):
                out[:, pl.ds((at // LANES * 4 + b) * LANES, LANES)] = block[b * COLS : (b + 1) * COLS]

    def product(i):
        return gram_of(held[i][5], PARTS[i], teams(i)[0].me, teams(i)[1].me, PARTS[i][2], off_all)

    zs.each(lambda index: small(zs, index, off_row, off_z.at[pl.ds(zs.me, 1)], 0))
    scatter_outer(0)
    scatter_outer(2)
    scatter_outer(1)
    scatter_outer(3)
    off_z[pl.ds(zs.me, 1)] = off_row[...]
    small_done(off_z.at[pl.ds(0, SIDE - 1)], 1, 0)
    for j in range(SIDE):
        off_plane[pl.ds(j, 1), :] = off_z[j]
    xy.each(lambda index: small(xy, index, off_plane, off_all.at[rows_at(xy.me, SIDE)], 1))
    off_all[rows_at(xy.me, SIDE), :] = off_plane[...]

    scatter_inner(2)
    scatter_inner(0)
    scatter_inner(3)
    scatter_inner(1)
    return_inner(0)
    return_inner(2)
    small_done(off_all.at[pl.ds(0, SIDE * (SIDE - 1))], 1, 1)
    total = product(0) + product(2)
    return_inner(1)
    return_inner(3)
    total = total + (product(1) + product(3))

    lane32 = lax.broadcasted_iota(jnp.int32, (COLS, LANES), 1) // COLS
    folded = tree_sum(
        jnp.where(lane32 == b, total[b * COLS : (b + 1) * COLS], 0.0) for b in range(4)
    )
    folded = folded + pltpu.roll(folded, 64, 1)
    folded = folded + pltpu.roll(folded, 32, 1)
    lane8 = lax.broadcasted_iota(jnp.int32, (8, LANES), 1) // COLS
    tile = tree_sum(
        jnp.where(lane8 == b, folded[b * 8 : (b + 1) * 8], 0.0) for b in range(4)
    )
    packed[...] = tile * (1.0 / TOTAL_SAMPLES)
    plane.each(lambda index: small(plane, index, packed, gram_plane.at[rows_at(plane.me, 8)], 2))
    gram_plane[rows_at(plane.me, 8), :] = packed[...]

    return_outer(0)
    return_outer(2)
    return_outer(1)

    small_done(gram_plane.at[pl.ds(0, 8 * (plane.count - 1))], 1, 2)
    gram_sum[...] = tree_sum(gram_plane[pl.ds(8 * j, 8), :] for j in range(plane.count))
    line.each(lambda index: small(line, index, gram_sum, gram_line.at[rows_at(line.me, 8)], 3))
    gram_line[rows_at(line.me, 8), :] = gram_sum[...]

    return_outer(3)
    finish(2)
    finish(0)
    finish(3)

    small_done(gram_line.at[pl.ds(0, 8 * (line.count - 1))], 1, 3)
    whole = tree_sum(gram_line[pl.ds(8 * j, 8), :] for j in range(line.count))
    for b in range(4):
        turned = pltpu.roll(whole, LANES - COLS * b, 1) if b else whole
        gram[pl.ds(b * 8, 8), :] = turned[:, :COLS]
    finish(1)

    picked = []
    for k in range(SAMPLES):
        at = offs[k]
        value = final[pl.ds((at // 512) * LANES + at % LANES, 1), :]
        picked.append(jnp.where(lane // COLS == (at // LANES) % 4, value, 0.0))
    picked = jnp.concatenate(picked, axis=0)
    picked = picked + pltpu.roll(picked, 64, 1)
    picked = picked + pltpu.roll(picked, 32, 1)
    sketch[...] = picked[:, :COLS]

    for i in range(len(PARTS)):
        for phase in range(4):
            sent(held[i][1], sems, 4 * i + phase, size(i))
    small_done(off_z.at[pl.ds(0, SIDE - 1)], 0, 0)
    small_done(off_all.at[pl.ds(0, SIDE * (SIDE - 1))], 0, 1)
    small_done(gram_plane.at[pl.ds(0, 8 * (plane.count - 1))], 0, 2)
    small_done(gram_line.at[pl.ds(0, 8 * (line.count - 1))], 0, 3)


def store(*refs):
    sems = refs[6]
    copies = []
    for i in range(3):
        copies.append(pltpu.make_async_copy(refs[i], refs[3 + i], sems.at[i]))
        copies[-1].start()
    for copy in copies:
        copy.wait()


def local(matrix_slab, sign_flips, sample_offset):
    f32 = jnp.float32
    scratch = [
        pltpu.VMEM((COLS, LOCAL), f32),
        pltpu.VMEM((LOCAL // LANES, LANES), jnp.int32),
        pltpu.SMEM((SAMPLES,), jnp.int32),
        pltpu.VMEM((ROWS, LANES), f32),
        pltpu.VMEM((ROWS, LANES), f32),
        pltpu.VMEM((1, 1, LANES), f32),
        pltpu.VMEM((SIDE, 1, LANES), f32),
        pltpu.VMEM((SIDE, LANES), f32),
        pltpu.VMEM((SIDE * SIDE, LANES), f32),
        pltpu.VMEM((8, LANES), f32),
        pltpu.VMEM((32 * 8, LANES), f32),
        pltpu.VMEM((8, LANES), f32),
        pltpu.VMEM((8 * 8, LANES), f32),
        pltpu.SemaphoreType.DMA((3,)),
        pltpu.SemaphoreType.DMA((2, 4 * len(PARTS))),
        pltpu.SemaphoreType.DMA((2, 4)),
    ]
    for _, count, _ in PARTS:
        scratch += [pltpu.VMEM((count, LANES), f32)] * 8
    shapes = (
        jax.ShapeDtypeStruct((COLS, LOCAL), f32),
        jax.ShapeDtypeStruct((SAMPLES, COLS), f32),
        jax.ShapeDtypeStruct((COLS, COLS), f32),
    )
    args = (matrix_slab, sign_flips.reshape(LOCAL // LANES, LANES), sample_offset)
    args = [pltpu.with_memory_space_constraint(arg, pltpu.HBM) for arg in args]
    results = pl.pallas_call(
        kernel,
        out_shape=shapes,
        in_specs=[pl.BlockSpec(memory_space=pl.ANY)] * 3,
        out_specs=[pl.BlockSpec(memory_space=pltpu.VMEM)] * 3,
        scratch_shapes=scratch,
        compiler_params=pltpu.CompilerParams(
            collective_id=0, has_side_effects=True, vmem_limit_bytes=24 << 20
        ),
        name="hadamard",
    )(*args)
    transformed, sketch, gram = pl.pallas_call(
        store,
        out_shape=shapes,
        in_specs=[pl.BlockSpec(memory_space=pl.ANY)] * 3,
        out_specs=[pl.BlockSpec(memory_space=pl.ANY)] * 3,
        scratch_shapes=[pltpu.SemaphoreType.DMA((3,))],
        compiler_params=pltpu.CompilerParams(vmem_limit_bytes=1 << 20),
        name="store",
    )(*(pltpu.with_memory_space_constraint(value, pltpu.VMEM) for value in results))
    return transformed, sketch.T, gram


def solution(mesh):
    return jax.shard_map(
        local,
        mesh=mesh,
        in_specs=(P(None, ("grp", "dev")), P(("grp", "dev")), P(("grp", "dev"))),
        out_specs=(P(None, ("grp", "dev")), P(None, ("grp", "dev")), P()),
        check_vma=False,
    )
```

time: 51.6 us -> 40.9 us (0.79)
  Pallas kernels: 46 us -> 40.1 us
  local copies, waits for them, and re-layouts: 4.47 us -> 0 us
    pallas_call x1 -> x2, Pallas kernels: 46 us -> 40.1 us  [the longest x1 39.3 us: local(): pl.pallas_call(kernel, out_shape=shapes, in_specs=[pl.BlockSpec(memory_sp...]
    unnamed x8 -> x0, local copies, waits for them, and re-layouts: 3.8 us -> none
    pallas_call x1 -> x0, local copies, waits for them, and re-layouts: 0.67 us -> none  [local(): pl.pallas_call(kernel, out_shape=(jax.ShapeDtypeStruct((COLS, LOCAL), f32...]
where the time goes in v2:
time: 40.9 us; the launch traced here: 40.8 us
  Pallas kernels  40.1 us (98%)
  between operations  0.64 us (2%)
    pallas_call x1, Pallas kernels, local(): pl.pallas_call(kernel, out_shape=shapes, in_specs=[pl.BlockSpec(memory_sp...  39.3 us
    pallas_call x1, Pallas kernels, local(): pl.pallas_call(store, out_shape=shapes, in_specs=[pl.BlockSpec(memory_spa...  0.83 us

profile of v2, /device:TPU:1, one launch (start us, length us, event | category | flops | bytes accessed | tf_op | source)
XLA Modules:
  0.0 40.8 jit_solution(18098977505082039415)
XLA Ops:
  0.6 39.3 %hadamard.1 = (f32[32,4096]{1,0:T(8,128)S(1)}, f32[16,32]{1,0:T(8,128)S(1)}, f32[32,32]{1,0:T(8,128)S(1)}) custom-call(f32[32,4096]{1,0:T(8,128)} %x_any.1, s32[32,128]{1,0:T(8,128)} %bitcast.2, s32[16]{0:T(128)} %offs_any.1), custom_call_target="tpu_custom_call" | custom-call | tf_op jit(solution)/shard_map/hadamard/pallas_call | solution.py:404
  40.0 0.8 %store.1 = (f32[32,4096]{1,0:T(8,128)}, f32[16,32]{1,0:T(8,128)}, f32[32,32]{1,0:T(8,128)}) custom-call(f32[32,4096]{1,0:T(8,128)S(1)} %get-tuple-element.9.refs_0_, f32[16,32]{1,0:T(8,128)S(1)} %get-tuple-element.10.refs_1_, f32[32,32]{1,0:T(8,128)S(1)} %get-tuple-element.11.refs_2_), custom_call_target="tpu_custom_call" | custom-call | tf_op jit(solution)/shard_map/store/pallas_call | solution.py:415

commit v3 on v2

--- a/solution.py
+++ b/solution.py
@@ -54,37 +54,39 @@
     return jnp.where(parity == 1, -scale, scale).astype(jnp.bfloat16)
 
 
+def wrap(value, count):
+    return jnp.where(value >= count, value - count, value)
+
+
 class Team:
     def __init__(self, grp, dev, kind):
         self.kind = kind
-        self.grp, self.high, self.low = grp, dev // 16, dev % 16
-        self.z, self.core = grp // 2 + 4 * self.high, grp % 2
+        self.high, self.low = lax.div(dev, 16), lax.rem(dev, 16)
+        self.grp, self.core = grp, lax.rem(grp, 2)
         self.me, self.count = {
-            "z": (2 * self.z + self.core, 16),
+            "z": (8 * self.high + grp, 16),
             "xy": (self.low, 16),
-            "plane": (16 * self.core + self.low, 32),
-            "line": (self.z, 8),
+            "line": (4 * self.high + lax.div(grp, 2), 8),
         }[kind]
 
     def device(self, index):
         if self.kind == "z":
-            return (index % 8, (index // 8) * 16 + self.low)
+            upper = index >= 8
+            return (jnp.where(upper, index - 8, index), jnp.where(upper, self.low + 16, self.low))
         if self.kind == "xy":
             return (self.grp, self.high * 16 + index)
-        if self.kind == "plane":
-            return ((self.grp // 2) * 2 + index // 16, self.high * 16 + index % 16)
-        return ((index % 4) * 2 + self.core, (index // 4) * 16 + self.low)
-
-    def peer(self, turn):
-        away = (turn + 1) // 2
-        return (self.me + self.count // 2 + away * (2 * ((turn + 1) % 2) - 1)) % self.count
+        upper = index >= 4
+        near = jnp.where(upper, index - 4, index)
+        return (near * 2 + self.core, jnp.where(upper, self.low + 16, self.low))
 
     def each(self, body):
         def step(turn, carry):
-            body(self.peer(turn))
+            away = lax.div(turn + 1, 2)
+            apart = self.count // 2 + away * (1 - 2 * lax.rem(turn, 2))
+            body(wrap(self.me + apart, self.count))
             return carry
 
-        lax.fori_loop(0, self.count - 1, step, 0)
+        lax.fori_loop(0, self.count - 1, step, 0, unroll=True)
 
 
 def rows_at(index, count):
@@ -179,11 +181,11 @@
 
 
 def kernel(x_any, flips_any, offs_any, out, sketch, gram, *scratch):
-    (x, flips, offs, mixed, final, off_row, off_z, off_plane, off_all, packed, gram_plane,
-     gram_sum, gram_line, load_sems, sems, small_sems) = scratch[:16]
-    held = [scratch[16 + 8 * i : 24 + 8 * i] for i in range(len(PARTS))]
+    (x, flips, offs, mixed, final, off_row, off_z, off_plane, off_all, packed, gram_xy,
+     gram_core, gram_sum, gram_line, load_sems, sems, small_sems) = scratch[:17]
+    held = [scratch[17 + 8 * i : 25 + 8 * i] for i in range(len(PARTS))]
     grp, dev = lax.axis_index("grp"), lax.axis_index("dev")
-    zs, xy, plane, line = (Team(grp, dev, kind) for kind in ("z", "xy", "plane", "line"))
+    zs, xy, line = (Team(grp, dev, kind) for kind in ("z", "xy", "line"))
 
     load_x = pltpu.make_async_copy(x_any, x, load_sems.at[0])
     load_f = pltpu.make_async_copy(flips_any, flips, load_sems.at[1])
@@ -193,7 +195,7 @@
     load_o.start()
 
     barrier = pltpu.get_barrier_semaphore()
-    for team in (zs, plane):
+    for team in (xy, zs):
         team.each(
             lambda index, team=team: pl.semaphore_signal(
                 barrier, inc=1, device_id=team.device(index), device_id_type=MESH
@@ -241,14 +243,7 @@
                 preferred_element_type=jnp.float32,
             )
 
-    load_o.wait()
-    lane = lax.broadcasted_iota(jnp.int32, (1, LANES), 1)
-    row = jnp.full((1, LANES), -1, jnp.int32)
-    for k in range(SAMPLES):
-        row = jnp.where(lane % COLS == k, offs[k], row)
-    off_row[...] = row.astype(jnp.float32)[None]
-
-    pl.semaphore_wait(barrier, zs.count + plane.count - 2)
+    pl.semaphore_wait(barrier, zs.count + xy.count - 2)
 
     def scatter_outer(i):
         exchange(teams(i)[0], held[i][0], held[i][1], sems, 4 * i, size(i))
@@ -284,30 +279,35 @@
     def product(i):
         return gram_of(held[i][5], PARTS[i], teams(i)[0].me, teams(i)[1].me, PARTS[i][2], off_all)
 
-    zs.each(lambda index: small(zs, index, off_row, off_z.at[pl.ds(zs.me, 1)], 0))
     scatter_outer(0)
     scatter_outer(2)
+    load_o.wait()
+    lane = lax.broadcasted_iota(jnp.int32, (1, LANES), 1)
+    row = jnp.full((1, LANES), -1, jnp.int32)
+    for k in range(SAMPLES):
+        row = jnp.where(lane % COLS == k, offs[k], row)
+    off_row[...] = row.astype(jnp.float32)[None]
+
+    zs.each(lambda index: small(zs, index, off_row, off_z.at[pl.ds(zs.me, 1)], 0))
     scatter_outer(1)
     scatter_outer(3)
     off_z[pl.ds(zs.me, 1)] = off_row[...]
+    scatter_inner(2)
+    scatter_inner(0)
     small_done(off_z.at[pl.ds(0, SIDE - 1)], 1, 0)
     for j in range(SIDE):
         off_plane[pl.ds(j, 1), :] = off_z[j]
     xy.each(lambda index: small(xy, index, off_plane, off_all.at[rows_at(xy.me, SIDE)], 1))
     off_all[rows_at(xy.me, SIDE), :] = off_plane[...]
 
-    scatter_inner(2)
-    scatter_inner(0)
     scatter_inner(3)
     scatter_inner(1)
+    return_inner(2)
     return_inner(0)
-    return_inner(2)
     small_done(off_all.at[pl.ds(0, SIDE * (SIDE - 1))], 1, 1)
-    total = product(0) + product(2)
+    return_inner(3)
     return_inner(1)
-    return_inner(3)
-    total = total + (product(1) + product(3))
-
+    total = product(0) + product(1) + product(2) + product(3)
     lane32 = lax.broadcasted_iota(jnp.int32, (COLS, LANES), 1) // COLS
     folded = tree_sum(
         jnp.where(lane32 == b, total[b * COLS : (b + 1) * COLS], 0.0) for b in range(4)
@@ -319,24 +319,29 @@
         jnp.where(lane8 == b, folded[b * 8 : (b + 1) * 8], 0.0) for b in range(4)
     )
     packed[...] = tile * (1.0 / TOTAL_SAMPLES)
-    plane.each(lambda index: small(plane, index, packed, gram_plane.at[rows_at(plane.me, 8)], 2))
-    gram_plane[rows_at(plane.me, 8), :] = packed[...]
+    xy.each(lambda index: small(xy, index, packed, gram_xy.at[rows_at(xy.me, 8)], 2))
+    gram_xy[rows_at(xy.me, 8), :] = packed[...]
 
     return_outer(0)
     return_outer(2)
+    small_done(gram_xy.at[pl.ds(0, 8 * (xy.count - 1))], 1, 2)
+    gram_core[pl.ds(0, 8), :] = tree_sum(gram_xy[pl.ds(8 * j, 8), :] for j in range(xy.count))
+    small(zs, zs.me + 1 - 2 * zs.core, gram_core.at[pl.ds(0, 8)], gram_core.at[pl.ds(8, 8)], 3)
+
     return_outer(1)
-
-    small_done(gram_plane.at[pl.ds(0, 8 * (plane.count - 1))], 1, 2)
-    gram_sum[...] = tree_sum(gram_plane[pl.ds(8 * j, 8), :] for j in range(plane.count))
-    line.each(lambda index: small(line, index, gram_sum, gram_line.at[rows_at(line.me, 8)], 3))
+    small_done(gram_core.at[pl.ds(8, 8)], 1, 3)
+    gram_sum[...] = gram_core[pl.ds(0, 8), :] + gram_core[pl.ds(8, 8), :]
+    line.each(lambda index: small(line, index, gram_sum, gram_line.at[rows_at(line.me, 8)], 4))
     gram_line[rows_at(line.me, 8), :] = gram_sum[...]
 
     return_outer(3)
     finish(2)
     finish(0)
     finish(3)
-
-    small_done(gram_line.at[pl.ds(0, 8 * (line.count - 1))], 1, 3)
+    for i in range(len(PARTS)):
+        for phase in range(3):
+            sent(held[i][1], sems, 4 * i + phase, size(i))
+    small_done(gram_line.at[pl.ds(0, 8 * (line.count - 1))], 1, 4)
     whole = tree_sum(gram_line[pl.ds(8 * j, 8), :] for j in range(line.count))
     for b in range(4):
         turned = pltpu.roll(whole, LANES - COLS * b, 1) if b else whole
@@ -354,12 +359,12 @@
     sketch[...] = picked[:, :COLS]
 
     for i in range(len(PARTS)):
-        for phase in range(4):
-            sent(held[i][1], sems, 4 * i + phase, size(i))
+        sent(held[i][1], sems, 4 * i + 3, size(i))
     small_done(off_z.at[pl.ds(0, SIDE - 1)], 0, 0)
     small_done(off_all.at[pl.ds(0, SIDE * (SIDE - 1))], 0, 1)
-    small_done(gram_plane.at[pl.ds(0, 8 * (plane.count - 1))], 0, 2)
-    small_done(gram_line.at[pl.ds(0, 8 * (line.count - 1))], 0, 3)
+    small_done(gram_xy.at[pl.ds(0, 8 * (xy.count - 1))], 0, 2)
+    small_done(gram_core.at[pl.ds(8, 8)], 0, 3)
+    small_done(gram_line.at[pl.ds(0, 8 * (line.count - 1))], 0, 4)
 
 
 def store(*refs):
@@ -385,12 +390,13 @@
         pltpu.VMEM((SIDE, LANES), f32),
         pltpu.VMEM((SIDE * SIDE, LANES), f32),
         pltpu.VMEM((8, LANES), f32),
-        pltpu.VMEM((32 * 8, LANES), f32),
+        pltpu.VMEM((SIDE * 8, LANES), f32),
+        pltpu.VMEM((2 * 8, LANES), f32),
         pltpu.VMEM((8, LANES), f32),
         pltpu.VMEM((8 * 8, LANES), f32),
         pltpu.SemaphoreType.DMA((3,)),
         pltpu.SemaphoreType.DMA((2, 4 * len(PARTS))),
-        pltpu.SemaphoreType.DMA((2, 4)),
+        pltpu.SemaphoreType.DMA((2, 5)),
     ]
     for _, count, _ in PARTS:
         scratch += [pltpu.VMEM((count, LANES), f32)] * 8

time: 40.9 us -> 39.8 us (0.973)
  Pallas kernels: 40.1 us -> 38.9 us
    pallas_call x1, Pallas kernels: 39.3 us -> 38.1 us  [local(): pl.pallas_call(kernel, out_shape=shapes, in_specs=[pl.BlockSpec(memory_sp...]
where the time goes in v3:
time: 39.8 us; the launch traced here: 39.6 us
  Pallas kernels  38.9 us (98%)
  between operations  0.64 us (2%)
    pallas_call x1, Pallas kernels, local(): pl.pallas_call(kernel, out_shape=shapes, in_specs=[pl.BlockSpec(memory_sp...  38.1 us
    pallas_call x1, Pallas kernels, local(): pl.pallas_call(store, out_shape=shapes, in_specs=[pl.BlockSpec(memory_spa...  0.83 us

profile of v3, /device:TPU:1, one launch (start us, length us, event | category | flops | bytes accessed | tf_op | source)
XLA Modules:
  0.0 39.6 jit_solution(17277914341127142226)
XLA Ops:
  0.6 38.1 %hadamard.1 = (f32[32,4096]{1,0:T(8,128)S(1)}, f32[16,32]{1,0:T(8,128)S(1)}, f32[32,32]{1,0:T(8,128)S(1)}) custom-call(f32[32,4096]{1,0:T(8,128)} %x_any.1, s32[32,128]{1,0:T(8,128)} %bitcast.2, s32[16]{0:T(128)} %offs_any.1), custom_call_target="tpu_custom_call" | custom-call | tf_op jit(solution)/shard_map/hadamard/pallas_call | solution.py:410
  38.8 0.8 %store.1 = (f32[32,4096]{1,0:T(8,128)}, f32[16,32]{1,0:T(8,128)}, f32[32,32]{1,0:T(8,128)}) custom-call(f32[32,4096]{1,0:T(8,128)S(1)} %get-tuple-element.9.refs_0_, f32[16,32]{1,0:T(8,128)S(1)} %get-tuple-element.10.refs_1_, f32[32,32]{1,0:T(8,128)S(1)} %get-tuple-element.11.refs_2_), custom_call_target="tpu_custom_call" | custom-call | tf_op jit(solution)/shard_map/store/pallas_call | solution.py:421

commit v4 on v3

--- a/solution.py
+++ b/solution.py
@@ -79,11 +79,18 @@
         near = jnp.where(upper, index - 4, index)
         return (near * 2 + self.core, jnp.where(upper, self.low + 16, self.low))
 
+    def partner(self, turn):
+        away = lax.div(turn + 1, 2)
+        apart = self.count // 2 + away * (1 - 2 * lax.rem(turn, 2))
+        return wrap(self.me + apart, self.count)
+
+    def ranked(self, turn):
+        index = jnp.where(turn < 8, turn + 1 - 2 * lax.rem(turn, 2), 23 - turn)
+        return jnp.where(self.me == index, 8, index)
+
     def each(self, body):
         def step(turn, carry):
-            away = lax.div(turn + 1, 2)
-            apart = self.count // 2 + away * (1 - 2 * lax.rem(turn, 2))
-            body(wrap(self.me + apart, self.count))
+            body(self.partner(turn))
             return carry
 
         lax.fori_loop(0, self.count - 1, step, 0, unroll=True)
@@ -93,20 +100,24 @@
     return pl.ds(pl.multiple_of(index * count, 8), count)
 
 
-def exchange(team, src, dst, sems, phase, size):
-    def one(index):
-        pltpu.make_async_remote_copy(
-            src_ref=src.at[rows_at(index, size)],
-            dst_ref=dst.at[rows_at(team.me, size)],
-            send_sem=sems.at[0, phase],
-            recv_sem=sems.at[1, phase],
-            device_id=team.device(index),
-            device_id_type=MESH,
-        ).start()
-
-    team.each(one)
-    mine = rows_at(team.me, size)
-    dst[mine, :] = src[mine, :]
+def exchange(sems, *jobs):
+    def step(turn, carry):
+        for team, src, dst, phase, size, ranked in jobs:
+            index = team.ranked(turn) if ranked else team.partner(turn)
+            pltpu.make_async_remote_copy(
+                src_ref=src.at[rows_at(index, size)],
+                dst_ref=dst.at[rows_at(team.me, size)],
+                send_sem=sems.at[0, phase],
+                recv_sem=sems.at[1, phase],
+                device_id=team.device(index),
+                device_id_type=MESH,
+            ).start()
+        return carry
+
+    lax.fori_loop(0, SIDE - 1, step, 0, unroll=True)
+    for team, src, dst, phase, size, _ in jobs:
+        mine = rows_at(team.me, size)
+        dst[mine, :] = src[mine, :]
 
 
 def arrived(dst, sems, phase, size):
@@ -152,24 +163,24 @@
 def gram_of(mid, part, first, outer, inner_along_z, offsets):
     start, count, _ = part
     size = count // SIDE
-    lane = lax.broadcasted_iota(jnp.int32, (8, LANES), 1)
-    marks = []
+    marks = [[] for _ in range(4)]
     for j in range(SIDE):
         for r in range(size // 16):
             row = start + first * size + outer * (size // 16) + r
-            place = ((row // LANES) * 4 + lane // COLS) * LANES + row % LANES
-            place = place.astype(jnp.float32)
+            place = lax.div(row, LANES) * 4 * LANES + lax.rem(row, LANES)
             for half in range(2):
                 if inner_along_z:
                     held = offsets[pl.ds(j * SIDE + half * 8, 8), :]
                 else:
                     held = offsets[pl.ds(j + half * 8 * SIDE, 8, stride=SIDE), :]
-                marks.append(jnp.where(held == place, 1.0, 0.0))
-    marks = jnp.concatenate(marks, axis=0).astype(jnp.bfloat16)
-    a = lax.broadcasted_iota(jnp.int32, (LANES, LANES), 0) // COLS
-    b = lax.broadcasted_iota(jnp.int32, (LANES, LANES), 1) // COLS
-    same = jnp.where(a == b, 1.0, 0.0).astype(jnp.bfloat16)
-    counts = jnp.dot(marks, same, preferred_element_type=jnp.float32)
+                for b in range(4):
+                    here = held == (place + b * LANES).astype(jnp.float32)
+                    marks[b].append(jnp.where(here, 1.0, 0.0))
+    marks = jnp.concatenate([jnp.concatenate(m, axis=0) for m in marks], axis=1)
+    a = lax.broadcasted_iota(jnp.int32, (4 * LANES, LANES), 0) // LANES
+    b = lax.broadcasted_iota(jnp.int32, (4 * LANES, LANES), 1) // COLS
+    spread = jnp.where(a == b, 1.0, 0.0).astype(jnp.bfloat16)
+    counts = jnp.dot(marks.astype(jnp.bfloat16), spread, preferred_element_type=jnp.float32)
     values = mid[...]
     return lax.dot_general(
         values,
@@ -181,21 +192,21 @@
 
 
 def kernel(x_any, flips_any, offs_any, out, sketch, gram, *scratch):
-    (x, flips, offs, mixed, final, off_row, off_z, off_plane, off_all, packed, gram_xy,
-     gram_core, gram_sum, gram_line, load_sems, sems, small_sems) = scratch[:17]
-    held = [scratch[17 + 8 * i : 25 + 8 * i] for i in range(len(PARTS))]
+    (x, flips, offs, mixed, final, off_row, off_z, off_plane, off_pairs, off_all, packed, gram_xy,
+     gram_core, gram_sum, gram_line, load_sems, sems, small_sems) = scratch[:18]
+    held = [scratch[18 + 8 * i : 26 + 8 * i] for i in range(len(PARTS))]
     grp, dev = lax.axis_index("grp"), lax.axis_index("dev")
     zs, xy, line = (Team(grp, dev, kind) for kind in ("z", "xy", "line"))
 
     load_x = pltpu.make_async_copy(x_any, x, load_sems.at[0])
     load_f = pltpu.make_async_copy(flips_any, flips, load_sems.at[1])
     load_o = pltpu.make_async_copy(offs_any, offs, load_sems.at[2])
-    load_f.start()
-    load_x.start()
-    load_o.start()
-
     barrier = pltpu.get_barrier_semaphore()
     for team in (xy, zs):
+        if team is zs:
+            load_f.start()
+            load_x.start()
+            load_o.start()
         team.each(
             lambda index, team=team: pl.semaphore_signal(
                 barrier, inc=1, device_id=team.device(index), device_id_type=MESH
@@ -246,27 +257,27 @@
     pl.semaphore_wait(barrier, zs.count + xy.count - 2)
 
     def scatter_outer(i):
-        exchange(teams(i)[0], held[i][0], held[i][1], sems, 4 * i, size(i))
+        return teams(i)[0], held[i][0], held[i][1], 4 * i, size(i), False
 
     def scatter_inner(i):
         _, got, flat, turned, got_inner, _, _, _ = held[i]
         arrived(got, sems, 4 * i, size(i))
         mix(got, flat, size(i))
         to_inner(flat, turned, size(i))
-        exchange(teams(i)[1], turned, got_inner, sems, 4 * i + 1, size(i))
+        return teams(i)[1], turned, got_inner, 4 * i + 1, size(i), False
 
     def return_inner(i):
         got_inner, mid, back = held[i][4:7]
         arrived(got_inner, sems, 4 * i + 1, size(i))
         mix(got_inner, mid, size(i))
-        exchange(teams(i)[1], mid, back, sems, 4 * i + 2, size(i))
+        return teams(i)[1], mid, back, 4 * i + 2, size(i), False
 
     def return_outer(i):
         back, flat = held[i][6:8]
         arrived(back, sems, 4 * i + 2, size(i))
         to_outer(back, flat, size(i))
         mine = final.at[pl.ds(PARTS[i][0], PARTS[i][1])]
-        exchange(teams(i)[0], flat, mine, sems, 4 * i + 3, size(i))
+        return teams(i)[0], flat, mine, 4 * i + 3, size(i), PARTS[i][2]
 
     def finish(i):
         start, count, _ = PARTS[i]
@@ -279,35 +290,40 @@
     def product(i):
         return gram_of(held[i][5], PARTS[i], teams(i)[0].me, teams(i)[1].me, PARTS[i][2], off_all)
 
-    scatter_outer(0)
-    scatter_outer(2)
+    exchange(sems, scatter_outer(0), scatter_outer(2))
     load_o.wait()
     lane = lax.broadcasted_iota(jnp.int32, (1, LANES), 1)
-    row = jnp.full((1, LANES), -1, jnp.int32)
+    row = jnp.zeros((1, LANES), jnp.int32)
     for k in range(SAMPLES):
-        row = jnp.where(lane % COLS == k, offs[k], row)
+        row = jnp.where(lane == k, offs[k], row)
     off_row[...] = row.astype(jnp.float32)[None]
 
     zs.each(lambda index: small(zs, index, off_row, off_z.at[pl.ds(zs.me, 1)], 0))
-    scatter_outer(1)
-    scatter_outer(3)
     off_z[pl.ds(zs.me, 1)] = off_row[...]
-    scatter_inner(2)
-    scatter_inner(0)
+    exchange(sems, scatter_outer(1), scatter_outer(3))
+    exchange(sems, scatter_inner(2))
+    exchange(sems, scatter_inner(0))
     small_done(off_z.at[pl.ds(0, SIDE - 1)], 1, 0)
+    for h in range(2):
+        off_plane[0, pl.ds(h, 1), :] = tree_sum(
+            pltpu.roll(off_z[8 * h + s], SAMPLES * s, 1) if s else off_z[8 * h] for s in range(8)
+        )
+    xy.each(lambda index: small(xy, index, off_plane, off_pairs.at[pl.ds(xy.me, 1)], 1))
+    off_pairs[pl.ds(xy.me, 1)] = off_plane[...]
+    exchange(sems, scatter_inner(3))
+    exchange(sems, scatter_inner(1))
+    exchange(sems, return_inner(2))
+    exchange(sems, return_inner(0))
+    exchange(sems, return_inner(3))
+    exchange(sems, return_inner(1))
+    small_done(off_pairs.at[pl.ds(0, SIDE - 1)], 1, 1)
+    own = lax.broadcasted_iota(jnp.int32, (8, LANES), 1) // SAMPLES
+    own = own == lax.broadcasted_iota(jnp.int32, (8, LANES), 0)
     for j in range(SIDE):
-        off_plane[pl.ds(j, 1), :] = off_z[j]
-    xy.each(lambda index: small(xy, index, off_plane, off_all.at[rows_at(xy.me, SIDE)], 1))
-    off_all[rows_at(xy.me, SIDE), :] = off_plane[...]
-
-    scatter_inner(3)
-    scatter_inner(1)
-    return_inner(2)
-    return_inner(0)
-    small_done(off_all.at[pl.ds(0, SIDE * (SIDE - 1))], 1, 1)
-    return_inner(3)
-    return_inner(1)
-    total = product(0) + product(1) + product(2) + product(3)
+        for h in range(2):
+            value = jnp.broadcast_to(off_pairs[j, pl.ds(h, 1), :], (8, LANES))
+            off_all[pl.ds(j * SIDE + h * 8, 8), :] = jnp.where(own, value, -1.0)
+    total = (product(0) + product(1)) + (product(2) + product(3))
     lane32 = lax.broadcasted_iota(jnp.int32, (COLS, LANES), 1) // COLS
     folded = tree_sum(
         jnp.where(lane32 == b, total[b * COLS : (b + 1) * COLS], 0.0) for b in range(4)
@@ -322,19 +338,19 @@
     xy.each(lambda index: small(xy, index, packed, gram_xy.at[rows_at(xy.me, 8)], 2))
     gram_xy[rows_at(xy.me, 8), :] = packed[...]
 
-    return_outer(0)
-    return_outer(2)
+    exchange(sems, return_outer(0))
+    exchange(sems, return_outer(2))
     small_done(gram_xy.at[pl.ds(0, 8 * (xy.count - 1))], 1, 2)
     gram_core[pl.ds(0, 8), :] = tree_sum(gram_xy[pl.ds(8 * j, 8), :] for j in range(xy.count))
     small(zs, zs.me + 1 - 2 * zs.core, gram_core.at[pl.ds(0, 8)], gram_core.at[pl.ds(8, 8)], 3)
 
-    return_outer(1)
+    exchange(sems, return_outer(1))
     small_done(gram_core.at[pl.ds(8, 8)], 1, 3)
     gram_sum[...] = gram_core[pl.ds(0, 8), :] + gram_core[pl.ds(8, 8), :]
     line.each(lambda index: small(line, index, gram_sum, gram_line.at[rows_at(line.me, 8)], 4))
     gram_line[rows_at(line.me, 8), :] = gram_sum[...]
 
-    return_outer(3)
+    exchange(sems, return_outer(3))
     finish(2)
     finish(0)
     finish(3)
@@ -361,7 +377,7 @@
     for i in range(len(PARTS)):
         sent(held[i][1], sems, 4 * i + 3, size(i))
     small_done(off_z.at[pl.ds(0, SIDE - 1)], 0, 0)
-    small_done(off_all.at[pl.ds(0, SIDE * (SIDE - 1))], 0, 1)
+    small_done(off_pairs.at[pl.ds(0, SIDE - 1)], 0, 1)
     small_done(gram_xy.at[pl.ds(0, 8 * (xy.count - 1))], 0, 2)
     small_done(gram_core.at[pl.ds(8, 8)], 0, 3)
     small_done(gram_line.at[pl.ds(0, 8 * (line.count - 1))], 0, 4)
@@ -387,7 +403,8 @@
         pltpu.VMEM((ROWS, LANES), f32),
         pltpu.VMEM((1, 1, LANES), f32),
         pltpu.VMEM((SIDE, 1, LANES), f32),
-        pltpu.VMEM((SIDE, LANES), f32),
+        pltpu.VMEM((1, 2, LANES), f32),
+        pltpu.VMEM((SIDE, 2, LANES), f32),
         pltpu.VMEM((SIDE * SIDE, LANES), f32),
         pltpu.VMEM((8, LANES), f32),
         pltpu.VMEM((SIDE * 8, LANES), f32),

time: 39.8 us -> 39.1 us (0.982)
  Pallas kernels: 38.9 us -> 38.3 us
    pallas_call x1, Pallas kernels: 38.1 us -> 37.5 us  [local(): pl.pallas_call(kernel, out_shape=shapes, in_specs=[pl.BlockSpec(memory_sp...]
where the time goes in v4:
time: 39.1 us; the launch traced here: 39 us
  Pallas kernels  38.3 us (98%)
  between operations  0.64 us (2%)
    pallas_call x1, Pallas kernels, local(): pl.pallas_call(kernel, out_shape=shapes, in_specs=[pl.BlockSpec(memory_sp...  37.5 us
    pallas_call x1, Pallas kernels, local(): pl.pallas_call(store, out_shape=shapes, in_specs=[pl.BlockSpec(memory_spa...  0.83 us

profile of v4, /device:TPU:1, one launch (start us, length us, event | category | flops | bytes accessed | tf_op | source)
XLA Modules:
  0.0 39.0 jit_solution(5993627917313873884)
XLA Ops:
  0.6 37.5 %hadamard.1 = (f32[32,4096]{1,0:T(8,128)S(1)}, f32[16,32]{1,0:T(8,128)S(1)}, f32[32,32]{1,0:T(8,128)S(1)}) custom-call(f32[32,4096]{1,0:T(8,128)} %x_any.1, s32[32,128]{1,0:T(8,128)} %bitcast.2, s32[16]{0:T(128)} %offs_any.1), custom_call_target="tpu_custom_call" | custom-call | tf_op jit(solution)/shard_map/hadamard/pallas_call | solution.py:427
  38.1 0.8 %store.1 = (f32[32,4096]{1,0:T(8,128)}, f32[16,32]{1,0:T(8,128)}, f32[32,32]{1,0:T(8,128)}) custom-call(f32[32,4096]{1,0:T(8,128)S(1)} %get-tuple-element.9.refs_0_, f32[16,32]{1,0:T(8,128)S(1)} %get-tuple-element.10.refs_1_, f32[32,32]{1,0:T(8,128)S(1)} %get-tuple-element.11.refs_2_), custom_call_target="tpu_custom_call" | custom-call | tf_op jit(solution)/shard_map/store/pallas_call | solution.py:438

commit v5 on v4

--- a/solution.py
+++ b/solution.py
@@ -277,7 +277,7 @@
         arrived(back, sems, 4 * i + 2, size(i))
         to_outer(back, flat, size(i))
         mine = final.at[pl.ds(PARTS[i][0], PARTS[i][1])]
-        return teams(i)[0], flat, mine, 4 * i + 3, size(i), PARTS[i][2]
+        return teams(i)[0], flat, mine, 4 * i + 3, size(i), i == 1
 
     def finish(i):
         start, count, _ = PARTS[i]
@@ -345,12 +345,12 @@
     small(zs, zs.me + 1 - 2 * zs.core, gram_core.at[pl.ds(0, 8)], gram_core.at[pl.ds(8, 8)], 3)
 
     exchange(sems, return_outer(1))
+    exchange(sems, return_outer(3))
     small_done(gram_core.at[pl.ds(8, 8)], 1, 3)
     gram_sum[...] = gram_core[pl.ds(0, 8), :] + gram_core[pl.ds(8, 8), :]
     line.each(lambda index: small(line, index, gram_sum, gram_line.at[rows_at(line.me, 8)], 4))
     gram_line[rows_at(line.me, 8), :] = gram_sum[...]
 
-    exchange(sems, return_outer(3))
     finish(2)
     finish(0)
     finish(3)

time: 39.1 us -> 39.2 us (level)
  no operation moved by 1% of the time
where the time goes in v5:
time: 39.2 us; the launch traced here: 39 us
  Pallas kernels  38.4 us (98%)
  between operations  0.64 us (2%)
    pallas_call x1, Pallas kernels, local(): pl.pallas_call(kernel, out_shape=shapes, in_specs=[pl.BlockSpec(memory_sp...  37.5 us
    pallas_call x1, Pallas kernels, local(): pl.pallas_call(store, out_shape=shapes, in_specs=[pl.BlockSpec(memory_spa...  0.83 us

profile of v5, /device:TPU:1, one launch (start us, length us, event | category | flops | bytes accessed | tf_op | source)
XLA Modules:
  0.0 39.0 jit_solution(2278581294395876596)
XLA Ops:
  0.6 37.5 %hadamard.1 = (f32[32,4096]{1,0:T(8,128)S(1)}, f32[16,32]{1,0:T(8,128)S(1)}, f32[32,32]{1,0:T(8,128)S(1)}) custom-call(f32[32,4096]{1,0:T(8,128)} %x_any.1, s32[32,128]{1,0:T(8,128)} %bitcast.2, s32[16]{0:T(128)} %offs_any.1), custom_call_target="tpu_custom_call" | custom-call | tf_op jit(solution)/shard_map/hadamard/pallas_call | solution.py:427
  38.2 0.8 %store.1 = (f32[32,4096]{1,0:T(8,128)}, f32[16,32]{1,0:T(8,128)}, f32[32,32]{1,0:T(8,128)}) custom-call(f32[32,4096]{1,0:T(8,128)S(1)} %get-tuple-element.9.refs_0_, f32[16,32]{1,0:T(8,128)S(1)} %get-tuple-element.10.refs_1_, f32[32,32]{1,0:T(8,128)S(1)} %get-tuple-element.11.refs_2_), custom_call_target="tpu_custom_call" | custom-call | tf_op jit(solution)/shard_map/store/pallas_call | solution.py:438

commit v6 on v5

--- a/solution.py
+++ b/solution.py
@@ -340,11 +340,11 @@
 
     exchange(sems, return_outer(0))
     exchange(sems, return_outer(2))
+    exchange(sems, return_outer(1))
     small_done(gram_xy.at[pl.ds(0, 8 * (xy.count - 1))], 1, 2)
     gram_core[pl.ds(0, 8), :] = tree_sum(gram_xy[pl.ds(8 * j, 8), :] for j in range(xy.count))
     small(zs, zs.me + 1 - 2 * zs.core, gram_core.at[pl.ds(0, 8)], gram_core.at[pl.ds(8, 8)], 3)
 
-    exchange(sems, return_outer(1))
     exchange(sems, return_outer(3))
     small_done(gram_core.at[pl.ds(8, 8)], 1, 3)
     gram_sum[...] = gram_core[pl.ds(0, 8), :] + gram_core[pl.ds(8, 8), :]

time: 39.2 us -> 39.8 us (1.015)
  Pallas kernels: 38.4 us -> 39 us
    pallas_call x1, Pallas kernels: 37.5 us -> 38.1 us  [local(): pl.pallas_call(kernel, out_shape=shapes, in_specs=[pl.BlockSpec(memory_sp...]
where the time goes in v6:
time: 39.8 us; the launch traced here: 39.6 us
  Pallas kernels  39 us (98%)
  between operations  0.64 us (2%)
    pallas_call x1, Pallas kernels, local(): pl.pallas_call(kernel, out_shape=shapes, in_specs=[pl.BlockSpec(memory_sp...  38.1 us
    pallas_call x1, Pallas kernels, local(): pl.pallas_call(store, out_shape=shapes, in_specs=[pl.BlockSpec(memory_spa...  0.83 us

profile of v6, /device:TPU:1, one launch (start us, length us, event | category | flops | bytes accessed | tf_op | source)
XLA Modules:
  0.0 39.6 jit_solution(15838130281703291503)
XLA Ops:
  0.6 38.1 %hadamard.1 = (f32[32,4096]{1,0:T(8,128)S(1)}, f32[16,32]{1,0:T(8,128)S(1)}, f32[32,32]{1,0:T(8,128)S(1)}) custom-call(f32[32,4096]{1,0:T(8,128)} %x_any.1, s32[32,128]{1,0:T(8,128)} %bitcast.2, s32[16]{0:T(128)} %offs_any.1), custom_call_target="tpu_custom_call" | custom-call | tf_op jit(solution)/shard_map/hadamard/pallas_call | solution.py:427
  38.8 0.8 %store.1 = (f32[32,4096]{1,0:T(8,128)}, f32[16,32]{1,0:T(8,128)}, f32[32,32]{1,0:T(8,128)}) custom-call(f32[32,4096]{1,0:T(8,128)S(1)} %get-tuple-element.9.refs_0_, f32[16,32]{1,0:T(8,128)S(1)} %get-tuple-element.10.refs_1_, f32[32,32]{1,0:T(8,128)S(1)} %get-tuple-element.11.refs_2_), custom_call_target="tpu_custom_call" | custom-call | tf_op jit(solution)/shard_map/store/pallas_call | solution.py:438
